TPU v7x, 32 devices: a whole 2x2x4 slice. The times are simulated.
32 devices in a mesh: stream: 2 (over core), dp: 4 (over y, x), tensor: 4 (over z).
Axes of the slice: x: 2, y: 2, z: 4, core: 2. Of those that a mesh axis runs over, the one named last changes fastest.
Arguments:
- hidden: bfloat16 [2, 64, 8192], P('stream', 'tensor', 'dp'), may hold values from -3 to 3
- cached_rotated_keys: bfloat16 [2, 64, 8, 256, 128], P('stream', 'dp', 'tensor'), may hold values from -6 to 6
- cached_values: bfloat16 [2, 64, 8, 256, 128], P('stream', 'dp', 'tensor'), may hold values from -18 to 18
- cache_lengths: int32 [2, 64], P('stream', 'dp'), may hold values from 1 to 256, as said below
- recent_ids: int32 [64, 128], replicated, may hold values from 0 to 8191
- guidance: float32 [64], replicated, may hold values from 1 to 3
- w_query: bfloat16 [8192, 8192], P('dp', 'tensor'), may hold values from -0.0625 to 0.0625
- key_value_weight: bfloat16 [8192, 2, 1024], P('dp', None, 'tensor'), may hold values from -0.0625 to 0.0625
- w_output: bfloat16 [8192, 8192], P('tensor', 'dp'), may hold values from -0.0625 to 0.0625
- norm_gain: bfloat16 [8192], P('dp'), may hold values from 0.5 to 1.5
- w_head: bfloat16 [8192, 8192], P(None, ('dp', 'tensor')), may hold values from -0.16503906 to 0.16503906
Outputs:
- guided_logprobs: float32 [64, 8192], P('stream', ('dp', 'tensor'))
Inputs may be any that keep to these rules, and one draw needn't show every extreme that they name: `cache_lengths`: every prompt has 1 to 256 filled slots in each stream; some prompt has all 256; lengths differ widely from one group of 16 prompts to the next.
All inputs are finite; a program needn't handle non-finite values.
Results may differ from a plain program's by a relative error of at most 0.0025.
Values may be sent and summed in bfloat16 or wider, within the bound.
No kernel may reach another device: no remote copies, remote signals or barrier semaphores. Data moves between devices by JAX's collectives and lax.ppermute only.
A program may use at most 64 MiB of HBM per device.

v0:
```python
import math

import jax
import jax.numpy as jnp
import numpy as np
from jax import lax
from jax.experimental import pallas as pl
from jax.experimental.pallas import tpu as pltpu
from jax.sharding import PartitionSpec as P

MODEL_WIDTH = 8192
HEAD_SIZE = 128


rope_theta = 500000.0
penalty_step = 1.5
norm_eps = 1e-05


def swap(value, axis, distance):
    if distance == 0:
        return value
    pairs = [(source, source ^ distance) for source in range(lax.axis_size(axis))]
    return lax.ppermute(value, axis, pairs)


def far_first(axis):
    return range(lax.axis_size(axis) - 1, -1, -1)


def gather_swapped(value, axis):
    return [swap(value, axis, distance) for distance in far_first(axis)]


def sum_totals(value, axes):
    count = lax.axis_size(axes)
    copies = jnp.broadcast_to(value[None], (count,) + value.shape)
    return jnp.sum(lax.all_to_all(copies, axes, 0, 0, tiled=True), 0)


def matmul_kernel(row_blocks, *refs):
    blocks, weights, out_ref = refs[:row_blocks], refs[row_blocks:-1], refs[-1]
    rows = jnp.concatenate([block[...] for block in blocks], axis=0)
    first = 0
    for weight in weights:
        last = first + weight.shape[1]
        product = jnp.dot(rows, weight[...], preferred_element_type=jnp.float32)
        out_ref[:, first:last] = product.astype(out_ref.dtype)
        first = last


def matmul(blocks, weights, dtype):
    rows = sum(block.shape[0] for block in blocks)
    cols = sum(weight.shape[1] for weight in weights)
    depth = weights[0].shape[0]
    whole = pl.BlockSpec(memory_space=pltpu.VMEM)
    return pl.pallas_call(
        lambda *refs: matmul_kernel(len(blocks), *refs),
        out_shape=jax.ShapeDtypeStruct((rows, cols), dtype),
        in_specs=[whole] * (len(blocks) + len(weights)),
        out_specs=whole,
        compiler_params=pltpu.CompilerParams(vmem_limit_bytes=8 * 1024 * 1024),
        cost_estimate=pl.CostEstimate(
            flops=2 * rows * cols * depth,
            bytes_accessed=2 * (depth * (rows + cols) + rows * cols),
            transcendentals=0,
        ),
    )(*blocks, *[pltpu.with_memory_space_constraint(weight, pltpu.VMEM) for weight in weights])


def head_kernel(places_ref, *refs):
    blocks, (weight_ref, penalty_ref, out_ref) = refs[:-3], refs[-3:]
    rows = jnp.concatenate([block[...] for block in blocks], axis=0)
    logits = jnp.dot(rows, weight_ref[...], preferred_element_type=jnp.float32)
    share = blocks[0].shape[0]
    for i in range(len(blocks)):
        place = pl.ds(pl.multiple_of(places_ref[i], 8), share)
        out_ref[place, :] = logits[i * share : (i + 1) * share] - penalty_ref[place, :]


def head(places, blocks, weight, penalty):
    whole = pl.BlockSpec(memory_space=pltpu.VMEM)
    rows, cols = penalty.shape
    depth = weight.shape[0]
    return pl.pallas_call(
        head_kernel,
        out_shape=jax.ShapeDtypeStruct((rows, cols), jnp.float32),
        in_specs=[pl.BlockSpec(memory_space=pltpu.SMEM)] + [whole] * (len(blocks) + 2),
        out_specs=whole,
        compiler_params=pltpu.CompilerParams(vmem_limit_bytes=8 * 1024 * 1024),
        cost_estimate=pl.CostEstimate(
            flops=2 * rows * cols * depth,
            bytes_accessed=2 * depth * (rows + cols) + 8 * rows * cols,
            transcendentals=0,
        ),
    )(places, *blocks, pltpu.with_memory_space_constraint(weight, pltpu.VMEM), penalty)


def load_kernel(weight_ref, out_ref, sems):
    pieces = sems.shape[0]
    rows = out_ref.shape[0] // pieces
    copies = []
    for piece in range(pieces):
        part = pl.ds(piece * rows, rows)
        copy = pltpu.make_async_copy(weight_ref.at[part], out_ref.at[part], sems.at[piece])
        copy.start()
        copies.append(copy)
    for copy in copies:
        copy.wait()


def load_to_vmem(weight):
    return pl.pallas_call(
        load_kernel,
        out_shape=pltpu.VMEM(weight.shape, weight.dtype),
        in_specs=[pl.BlockSpec(memory_space=pltpu.HBM)],
        out_specs=pl.BlockSpec(memory_space=pltpu.VMEM),
        scratch_shapes=[pltpu.SemaphoreType.DMA((4,))],
        compiler_params=pltpu.CompilerParams(vmem_limit_bytes=8 * 1024 * 1024),
        cost_estimate=pl.CostEstimate(
            flops=0, bytes_accessed=4 * weight.size, transcendentals=0
        ),
    )(pltpu.with_memory_space_constraint(weight, pltpu.HBM))


def load_projections_kernel(query_ref, pair_ref, query_out, pair_out, pair_raw, sems):
    pieces = sems.shape[0] - 1
    depth, members, cols = pair_raw.shape
    rows = depth // pieces
    step = math.gcd(rows, 256)
    copies = []
    for piece in range(pieces):
        part = pl.ds(piece * rows, rows)
        copy = pltpu.make_async_copy(pair_ref.at[part], pair_raw.at[part], sems.at[piece])
        copy.start()
        copies.append(copy)
    query_copy = pltpu.make_async_copy(query_ref, query_out, sems.at[pieces])
    query_copy.start()
    for piece in range(pieces):
        copies[piece].wait()

        def relayout(index, carry, first=piece * rows):
            part = pl.ds(pl.multiple_of(first + index * step, step), step)
            for member in range(members):
                pair_out[part, member * cols : (member + 1) * cols] = pair_raw[part, member, :]
            return carry

        lax.fori_loop(0, rows // step, relayout, 0)
    query_copy.wait()


def load_projections(query, pair):
    depth, members, cols = pair.shape
    arrays = [pltpu.with_memory_space_constraint(array, pltpu.HBM) for array in (query, pair)]
    return pl.pallas_call(
        load_projections_kernel,
        out_shape=(
            pltpu.VMEM(query.shape, query.dtype),
            pltpu.VMEM((depth, members * cols), pair.dtype),
        ),
        in_specs=[pl.BlockSpec(memory_space=pltpu.HBM)] * 2,
        out_specs=[pl.BlockSpec(memory_space=pltpu.VMEM)] * 2,
        scratch_shapes=[pltpu.VMEM(pair.shape, pair.dtype), pltpu.SemaphoreType.DMA((5,))],
        compiler_params=pltpu.CompilerParams(vmem_limit_bytes=16 * 1024 * 1024),
        cost_estimate=pl.CostEstimate(
            flops=0, bytes_accessed=4 * (query.size + pair.size), transcendentals=0
        ),
    )(*arrays)


def rotation(positions):
    halfway = HEAD_SIZE // 2
    frequency = np.asarray(rope_theta ** (-np.arange(halfway) * 2.0 / HEAD_SIZE), np.float32)
    angles = positions.astype(jnp.float32)[:, None, None] * frequency
    return jnp.cos(angles), jnp.sin(angles)


def rotate(values, cosine_term, sine_term):
    halfway = values.shape[-1] // 2
    first_half = values[..., :halfway]
    second_half = values[..., halfway:]
    return jnp.concatenate(
        [
            first_half * cosine_term - second_half * sine_term,
            second_half * cosine_term + first_half * sine_term,
        ],
        axis=-1,
    )


def repeat_counts(recent_ids, first_column, width):
    columns = first_column + jnp.arange(width, dtype=jnp.int32)
    return jnp.sum((recent_ids[:, :, None] == columns[None, None, :]).astype(jnp.float32), 1)


def body(
    hidden,
    cached_rotated_keys,
    cached_values,
    cache_lengths,
    recent_ids,
    guidance,
    w_query,
    key_value_weight,
    w_output,
    norm_gain,
    w_head,
):
    streams, dps, tensors = (lax.axis_size(axis) for axis in ("stream", "dp", "tensor"))
    stream, dp, tensor = (lax.axis_index(axis) for axis in ("stream", "dp", "tensor"))
    local_width = hidden.shape[2]
    query_cols = w_query.shape[1]
    kv_cols = key_value_weight.shape[2]
    local_prompts = cache_lengths.shape[1]
    hidden_prompts = hidden.shape[1]
    prompts = recent_ids.shape[0]
    lengths = cache_lengths[0]
    vocab_local = w_head.shape[1]

    hidden_blocks = gather_swapped(hidden[0], "tensor")
    all_rows = jnp.concatenate(hidden_blocks, axis=0)
    w_query, key_value_weight, stream, dp, tensor = lax.optimization_barrier(
        (w_query, key_value_weight, stream, dp, tensor)
    )
    projected_parts = matmul(
        hidden_blocks, load_projections(w_query, key_value_weight), jnp.bfloat16
    )
    (projected_parts, lengths, recent_ids, guidance, norm_gain, stream, dp, tensor) = (
        lax.optimization_barrier(
            (projected_parts, lengths, recent_ids, guidance, norm_gain, stream, dp, tensor)
        )
    )
    column_base = (dp * tensors + tensor) * vocab_local
    cosine_term, sine_term = rotation(lengths)

    def hidden_place(prompt):
        block = prompt // hidden_prompts
        return (tensors - 1 - (tensor ^ block)) * hidden_prompts + prompt % hidden_prompts

    gain_rows = norm_gain.reshape(local_prompts, -1)
    total_cols = query_cols + 2 * kv_cols
    projected, gain_blocks = 0.0, []
    for distance in far_first("dp"):
        sending = lax.dynamic_slice_in_dim(
            projected_parts, hidden_place((dp ^ distance) * local_prompts), local_prompts, 0
        )
        arrived = swap(jnp.concatenate([sending, gain_rows], axis=1), "dp", distance)
        projected = projected + arrived[:, :total_cols].astype(jnp.float32)
        gain_blocks.append(arrived[:, total_cols:].reshape(local_width))
    gain = jnp.zeros((local_width * dps,), norm_gain.dtype)
    for distance, block in zip(far_first("dp"), gain_blocks):
        gain = lax.dynamic_update_slice_in_dim(gain, block, (dp ^ distance) * local_width, 0)

    query_heads = query_cols // HEAD_SIZE
    kv_heads = kv_cols // HEAD_SIZE
    rotated_query = rotate(
        projected[:, :query_cols].reshape(local_prompts, query_heads, HEAD_SIZE),
        cosine_term,
        sine_term,
    ).astype(jnp.bfloat16)
    key_value_rows = projected[:, query_cols:].reshape(local_prompts, 2, kv_heads, HEAD_SIZE)
    fresh_key = rotate(key_value_rows[:, 0], cosine_term, sine_term).astype(jnp.bfloat16)
    value_new = key_value_rows[:, 1].astype(jnp.bfloat16)
    grouped_queries = rotated_query.reshape(
        local_prompts, kv_heads, query_heads // kv_heads, HEAD_SIZE
    )
    attention_scale = HEAD_SIZE ** (-0.5)
    key_block = cached_rotated_keys[0]
    value_block = cached_values[0]
    scores = (
        jnp.einsum(
            "pkgd,pksd->pkgs", grouped_queries, key_block, preferred_element_type=jnp.float32
        )
        * attention_scale
    )
    self_score = (
        jnp.einsum("pkgd,pkd->pkg", grouped_queries, fresh_key, preferred_element_type=jnp.float32)
        * attention_scale
    )
    valid = jnp.arange(key_block.shape[2], dtype=jnp.int32)[None, :] < lengths[:, None]
    exps = jnp.where(valid[:, None, None, :], jnp.exp(scores), 0.0)
    own_exp = jnp.exp(self_score)
    denominator = jnp.sum(exps, -1) + own_exp
    weights = (exps / denominator[..., None]).astype(jnp.bfloat16)
    own_weight = (own_exp / denominator).astype(jnp.bfloat16)
    attended = jnp.einsum(
        "pkgs,pksd->pkgd", weights, value_block, preferred_element_type=jnp.float32
    )
    attended = (
        attended
        + own_weight.astype(jnp.float32)[..., None] * value_new.astype(jnp.float32)[:, :, None, :]
    )
    attended = attended.reshape(local_prompts, query_cols).astype(jnp.bfloat16)

    half = prompts // streams
    recent_mine = lax.dynamic_slice_in_dim(recent_ids, stream * half, half, 0)
    penalty = penalty_step * repeat_counts(recent_mine, column_base, vocab_local)
    attended, penalty = lax.optimization_barrier((attended, penalty))

    attended_blocks = gather_swapped(attended, "dp")
    w_output, _ = lax.optimization_barrier((w_output, attended))
    partial_out = matmul(attended_blocks, [load_to_vmem(w_output)], jnp.bfloat16)

    share = half // tensors

    def partial_rows(tensor_to):
        parts = []
        for other in range(streams):
            prompt = (stream ^ other) * half + tensor_to * share
            block = dps - 1 - (dp ^ (prompt // local_prompts))
            place = block * local_prompts + prompt % local_prompts
            parts.append(lax.dynamic_slice_in_dim(partial_out, place, share, 0))
        return jnp.concatenate(parts, axis=0)

    def hidden_rows(stream_to):
        place = hidden_place(stream_to * half + tensor * share)
        return lax.dynamic_slice_in_dim(all_rows, place, share, 0).astype(jnp.float32)

    summed = jnp.concatenate([hidden_rows(stream ^ other) for other in range(streams)], axis=0)
    for distance in far_first("tensor"):
        arrived = swap(partial_rows(tensor ^ distance), "tensor", distance)
        summed = summed + arrived.astype(jnp.float32)
    residuals = summed.astype(jnp.bfloat16).reshape(streams, share, local_width)
    pair = [swap(residuals[other], "stream", other) for other in range(streams)]
    pair = jnp.concatenate(pair, axis=0)

    whole = jnp.zeros((streams * share, local_width * dps), jnp.bfloat16)
    for distance, block in zip(far_first("dp"), gather_swapped(pair, "dp")):
        whole = lax.dynamic_update_slice_in_dim(whole, block, (dp ^ distance) * local_width, 1)
    whole = whole.reshape(streams, share, -1).astype(jnp.float32)
    inverse = lax.rsqrt(jnp.sum(whole * whole, 2) / MODEL_WIDTH + norm_eps)
    guide = lax.dynamic_slice_in_dim(guidance, stream * half + tensor * share, share, 0)
    own_guide = jnp.where(stream == 0, guide, 1.0 - guide)
    factors = inverse * jnp.stack([own_guide, 1.0 - own_guide])
    mixed = jnp.sum(whole * factors[:, :, None], 0) * gain.astype(jnp.float32)
    mixed = mixed.astype(jnp.bfloat16)

    mixed_blocks = [swap(mixed, "tensor", distance) for distance in range(tensors)]
    w_head, _ = lax.optimization_barrier((w_head, mixed))
    places = jnp.stack([(tensor ^ distance) * share for distance in range(tensors)])
    guided = head(places.astype(jnp.int32), mixed_blocks, load_to_vmem(w_head), penalty)
    totals = sum_totals(jnp.sum(jnp.exp(guided), 1), ("dp", "tensor"))
    return guided - jnp.log(totals)[:, None]


def solution(mesh):
    return jax.shard_map(
        body,
        mesh=mesh,
        in_specs=(
            P("stream", "tensor", "dp"),
            P("stream", "dp", "tensor", None, None),
            P("stream", "dp", "tensor", None, None),
            P("stream", "dp"),
            P(),
            P(),
            P("dp", "tensor"),
            P("dp", None, "tensor"),
            P("tensor", "dp"),
            P("dp"),
            P(None, ("dp", "tensor")),
        ),
        out_specs=P("stream", ("dp", "tensor")),
        check_vma=False,
    )
```

profile of v0, /device:TPU:0, one launch (start us, length us, event | category | flops | bytes accessed | tf_op | source)
XLA Modules:
  0.0 78.8 jit_solution(7722864449204885031)
XLA Ops:
  0.0 5.0 %collective-permute-start = (bf16[16,2048]{1,0:T(8,128)(2,1)}, bf16[16,2048]{1,0:T(8,128)(2,1)S(1)}, u32[]{:S(2)}, u32[]{:S(2)}) collective-permute-start(bf16[16,2048]{1,0:T(8,128)(2,1)} %bitcast.74), channel_id=1, source_target_pairs={{0,3},{1,2},{2,1},{3,0},{4,7},{5,6},{6,5},{7,4},{8,11},{9,10},{10,... | collective-permute-start | bytes 196616 | tf_op jit(solution)/shard_map/ppermute | solution.py:24
  5.7 5.5 %shard_map.118 = (bf16[2048,2048]{1,0:T(8,128)(2,1)S(1)}, bf16[2048,512]{1,0:T(8,128)(2,1)S(1)}) custom-call(bf16[2048,2048]{1,0:T(8,128)(2,1)} %query_ref, bf16[2048,2,256]{2,1,0:T(2,128)(2,1)} %pair_ref), custom_call_target="tpu_custom_call" | custom-call | bytes 20971520 | tf_op jit(solution)/shard_map/pallas_call | solution.py:155
  11.3 1.9 %shard_map.119 = bf16[64,2560]{1,0:T(8,128)(2,1)S(1)} custom-call(bf16[16,2048]{1,0:T(8,128)(2,1)S(1)} %collective-permute-done.refs_0_, bf16[16,2048]{1,0:T(8,128)(2,1)S(1)} %collective-permute-done.1.refs_1_, bf16[16,2048]{1,0:T(8,128)(2,1)S(1)} %collective-permute-done.2.refs_2_, bf16[16,2048]{1,0:T(8,128)(2,1)S(1)} %bitcast.77, ...), custom_call_target="tpu_custom_call" | custom-call | flops 671088640 | bytes 11075584 | tf_op jit(solution)/shard_map/pallas_call | solution.py:57
  13.6 2.7 %collective-permute-start.3 = (bf16[16,2688]{1,0:T(8,128)(2,1)S(1)}, bf16[16,2688]{1,0:T(8,128)(2,1)S(1)}, u32[]{:S(2)}, u32[]{:S(2)}) collective-permute-start(bf16[16,2688]{1,0:T(8,128)(2,1)S(1)} %get-tuple-element.66), channel_id=1, source_target_pairs={{0,12},{4,8},{8,4},{12,0},{1,13},{5,9},{9,5},{13,1},{2,14},{6,10},... | collective-permute-start | bytes 258056 | tf_op jit(solution)/shard_map/ppermute | solution.py:24
  17.1 1.2 %convert_reduce_fusion = f32[32,512]{1,0:T(8,128)S(1)} fusion(s32[512]{0:T(512)S(1)} %iota_add_fusion, s32[32,128]{1,0:T(8,128)S(1)} %constant_dynamic-slice_fusion.8), kind=kLoop, calls=%fused_computation | loop fusion | flops 6275072 | bytes 83968 | tf_op jit(solution)/shard_map/reduce_sum | solution.py:193
  19.1 1.6 %collective-permute-done.4 = bf16[16,2688]{1,0:T(8,128)(2,1)S(1)} collective-permute-done((bf16[16,2688]{1,0:T(8,128)(2,1)S(1)}, bf16[16,2688]{1,0:T(8,128)(2,1)S(1)}, u32[]{:S(2)}, u32[]{:S(2)}) %collective-permute-start.4) | collective-permute-done | bytes 86048 | tf_op jit(solution)/shard_map/ppermute | solution.py:24
  23.4 1.6 %collective-permute-start.6 = (bf16[16,2048]{1,0:T(8,128)(2,1)S(1)}, bf16[16,2048]{1,0:T(8,128)(2,1)S(1)}, u32[]{:S(2)}, u32[]{:S(2)}) collective-permute-start(bf16[16,2048]{1,0:T(8,128)(2,1)S(1)} %bitcast.70), channel_id=1, source_target_pairs={{0,12},{4,8},{8,4},{12,0},{1,13},{5,9},{9,5},{13,1},{2,14},{6,10},... | collective-permute-start | bytes 196616 | tf_op jit(solution)/shard_map/ppermute | solution.py:24
  25.6 1.4 %collective-permute-start.8 = (bf16[16,2048]{1,0:T(8,128)(2,1)S(1)}, bf16[16,2048]{1,0:T(8,128)(2,1)S(1)}, u32[]{:S(2)}, u32[]{:S(2)}) collective-permute-start(bf16[16,2048]{1,0:T(8,128)(2,1)S(1)} %bitcast.72), channel_id=1, source_target_pairs={{0,4},{4,0},{8,12},{12,8},{1,5},{5,1},{9,13},{13,9},{2,6},{6,2},{1... | collective-permute-start | bytes 196616 | tf_op jit(solution)/shard_map/ppermute | solution.py:24
  27.0 3.5 %shard_map.120.refs_4_ = bf16[2048,2048]{1,0:T(8,128)(2,1)S(1)} custom-call(bf16[2048,2048]{1,0:T(8,128)(2,1)} %weight_ref), custom_call_target="tpu_custom_call" | custom-call | bytes 16777216 | tf_op jit(solution)/shard_map/pallas_call | solution.py:113
  30.6 1.6 %shard_map.121 = bf16[64,2048]{1,0:T(8,128)(2,1)S(1)} custom-call(bf16[16,2048]{1,0:T(8,128)(2,1)S(1)} %collective-permute-done.6.refs_0_, bf16[16,2048]{1,0:T(8,128)(2,1)S(1)} %collective-permute-done.7.refs_1_, bf16[16,2048]{1,0:T(8,128)(2,1)S(1)} %collective-permute-done.8.refs_2_, bf16[16,2048]{1,0:T(8,128)(2,1)S(1)} %bitcast.73, ...), custom_call_target="tpu_custom_call" | custom-call | flops 536870912 | bytes 8912896 | tf_op jit(solution)/shard_map/pallas_call | solution.py:57
  32.3 3.7 %collective-permute-start.9 = (bf16[16,2048]{1,0:T(8,128)(2,1)S(1)}, bf16[16,2048]{1,0:T(8,128)(2,1)S(1)}, u32[]{:S(2)}, u32[]{:S(2)}) collective-permute-start(bf16[16,2048]{1,0:T(8,128)(2,1)S(1)} %pad_maximum_fusion.5), channel_id=1, source_target_pairs={{0,3},{1,2},{2,1},{3,0},{4,7},{5,6},{6,5},{7,4},{8,11},{9,10},{10,... | collective-permute-start | bytes 196616 | tf_op jit(solution)/shard_map/ppermute | solution.py:24
  36.8 2.2 %collective-permute-done.9 = bf16[16,2048]{1,0:T(8,128)(2,1)S(1)} collective-permute-done((bf16[16,2048]{1,0:T(8,128)(2,1)S(1)}, bf16[16,2048]{1,0:T(8,128)(2,1)S(1)}, u32[]{:S(2)}, u32[]{:S(2)}) %collective-permute-start.9) | collective-permute-done | bytes 65568 | tf_op jit(solution)/shard_map/ppermute | solution.py:24
  39.0 2.2 %collective-permute-done.10 = bf16[16,2048]{1,0:T(8,128)(2,1)S(1)} collective-permute-done((bf16[16,2048]{1,0:T(8,128)(2,1)S(1)}, bf16[16,2048]{1,0:T(8,128)(2,1)S(1)}, u32[]{:S(2)}, u32[]{:S(2)}) %collective-permute-start.10) | collective-permute-done | bytes 65568 | tf_op jit(solution)/shard_map/ppermute | solution.py:24
  41.3 1.2 %collective-permute-done.12 = bf16[8,2048]{1,0:T(8,128)(2,1)S(1)} collective-permute-done((bf16[8,2048]{1,0:T(8,128)(2,1)S(1)}, bf16[8,2048]{1,0:T(8,128)(2,1)S(1)}, u32[]{:S(2)}, u32[]{:S(2)}) %collective-permute-start.12) | collective-permute-done | bytes 32800 | tf_op jit(solution)/shard_map/ppermute | solution.py:24
  42.5 1.6 %collective-permute-start.13 = (bf16[16,2048]{1,0:T(8,128)(2,1)S(1)}, bf16[16,2048]{1,0:T(8,128)(2,1)S(1)}, u32[]{:S(2)}, u32[]{:S(2)}) collective-permute-start(bf16[16,2048]{1,0:T(8,128)(2,1)S(1)} %pad_maximum_fusion.8), channel_id=1, source_target_pairs={{0,12},{4,8},{8,4},{12,0},{1,13},{5,9},{9,5},{13,1},{2,14},{6,10},... | collective-permute-start | bytes 196616 | tf_op jit(solution)/shard_map/ppermute | solution.py:24
  44.8 1.4 %collective-permute-start.15 = (bf16[16,2048]{1,0:T(8,128)(2,1)S(1)}, bf16[16,2048]{1,0:T(8,128)(2,1)S(1)}, u32[]{:S(2)}, u32[]{:S(2)}) collective-permute-start(bf16[16,2048]{1,0:T(8,128)(2,1)S(1)} %pad_maximum_fusion.8), channel_id=1, source_target_pairs={{0,4},{4,0},{8,12},{12,8},{1,5},{5,1},{9,13},{13,9},{2,6},{6,2},{1... | collective-permute-start | bytes 196616 | tf_op jit(solution)/shard_map/ppermute | solution.py:24
  46.2 1.5 %collective-permute-done.13 = bf16[16,2048]{1,0:T(8,128)(2,1)S(1)} collective-permute-done((bf16[16,2048]{1,0:T(8,128)(2,1)S(1)}, bf16[16,2048]{1,0:T(8,128)(2,1)S(1)}, u32[]{:S(2)}, u32[]{:S(2)}) %collective-permute-start.13) | collective-permute-done | bytes 65568 | tf_op jit(solution)/shard_map/ppermute | solution.py:24
  47.8 1.2 %collective-permute-done.14 = bf16[16,2048]{1,0:T(8,128)(2,1)S(1)} collective-permute-done((bf16[16,2048]{1,0:T(8,128)(2,1)S(1)}, bf16[16,2048]{1,0:T(8,128)(2,1)S(1)}, u32[]{:S(2)}, u32[]{:S(2)}) %collective-permute-start.14) | collective-permute-done | bytes 65568 | tf_op jit(solution)/shard_map/ppermute | solution.py:24
  50.2 1.7 %collective-permute-start.17 = (bf16[8,8192]{1,0:T(8,128)(2,1)S(1)}, bf16[8,8192]{1,0:T(8,128)(2,1)S(1)}, u32[]{:S(2)}, u32[]{:S(2)}) collective-permute-start(bf16[8,8192]{1,0:T(8,128)(2,1)S(1)} %multiply_convert_fusion.refs_0_), channel_id=1, source_target_pairs={{0,2},{1,3},{2,0},{3,1},{4,6},{5,7},{6,4},{7,5},{8,10},{9,11},{10,... | collective-permute-start | bytes 393224 | tf_op jit(solution)/shard_map/ppermute | solution.py:24
  51.9 2.2 %collective-permute-start.18 = (bf16[8,8192]{1,0:T(8,128)(2,1)S(1)}, bf16[8,8192]{1,0:T(8,128)(2,1)S(1)}, u32[]{:S(2)}, u32[]{:S(2)}) collective-permute-start(bf16[8,8192]{1,0:T(8,128)(2,1)S(1)} %multiply_convert_fusion.refs_0_), channel_id=1, source_target_pairs={{0,3},{1,2},{2,1},{3,0},{4,7},{5,6},{6,5},{7,4},{8,11},{9,10},{10,... | collective-permute-start | bytes 393224 | tf_op jit(solution)/shard_map/ppermute | solution.py:24
  54.1 3.5 %shard_map.122.refs_4_ = bf16[8192,512]{1,0:T(8,128)(2,1)S(1)} custom-call(bf16[8192,512]{1,0:T(8,128)(2,1)} %weight_ref.1), custom_call_target="tpu_custom_call" | custom-call | bytes 16777216 | tf_op jit(solution)/shard_map/pallas_call | solution.py:113
  57.7 5.3 %collective-permute-done.17.refs_2_ = bf16[8,8192]{1,0:T(8,128)(2,1)S(1)} collective-permute-done((bf16[8,8192]{1,0:T(8,128)(2,1)S(1)}, bf16[8,8192]{1,0:T(8,128)(2,1)S(1)}, u32[]{:S(2)}, u32[]{:S(2)}) %collective-permute-start.17) | collective-permute-done | bytes 131104 | tf_op jit(solution)/shard_map/ppermute | solution.py:24
  62.9 2.1 %shard_map.123 = f32[32,512]{1,0:T(8,128)S(1)} custom-call(s32[4]{0:T(128)S(1)} %pad_add_fusion.places_ref, bf16[8,8192]{1,0:T(8,128)(2,1)S(1)} %multiply_convert_fusion.refs_0_, bf16[8,8192]{1,0:T(8,128)(2,1)S(1)} %collective-permute-done.16.refs_1_, bf16[8,8192]{1,0:T(8,128)(2,1)S(1)} %collective-permute-done.17.refs_2_, ...), custom_call_target="tpu_custom_call" | custom-call | flops 268435456 | bytes 9043968 | tf_op jit(solution)/shard_map/pallas_call | solution.py:85
  65.1 12.9 %all_to_all.6 = f32[16,1,32]{2,1,0:T(1,128)S(1)} all-to-all(f32[16,1,32]{2,1,0:T(1,128)S(1)} %broadcast_in_dim.22), channel_id=1, replica_groups=mesh['stream'=2,'dp'=4,'tensor'=4] {'dp','tensor'}, dimensions={0} | all-to-all | bytes 4096 | tf_op jit(solution)/shard_map/all_to_all | solution.py:38
  (94 shorter events, 9.5 us)
Async XLA Ops:
  0.0 21.9 %copy-start = (bf16[1,16,2,256,128]{4,3,2,1,0:T(8,128)(2,1)S(1)}, bf16[1,16,2,256,128]{4,3,2,1,0:T(8,128)(2,1)}, u32[]{:S(2)}) copy-start(bf16[1,16,2,256,128]{4,3,2,1,0:T(8,128)(2,1)} %param.13) | copy-start | bytes 6291460
  0.0 11.2 %collective-permute-start = (bf16[16,2048]{1,0:T(8,128)(2,1)}, bf16[16,2048]{1,0:T(8,128)(2,1)S(1)}, u32[]{:S(2)}, u32[]{:S(2)}) collective-permute-start(bf16[16,2048]{1,0:T(8,128)(2,1)} %bitcast.74), channel_id=1, source_target_pairs={{0,3},{1,2},{2,1},{3,0},{4,7},{5,6},{6,5},{7,4},{8,11},{9,10},{10,... | collective-permute-start | bytes 196616 | tf_op jit(solution)/shard_map/ppermute | solution.py:24
  5.1 6.2 %collective-permute-start.1 = (bf16[16,2048]{1,0:T(8,128)(2,1)}, bf16[16,2048]{1,0:T(8,128)(2,1)S(1)}, u32[]{:S(2)}, u32[]{:S(2)}) collective-permute-start(bf16[16,2048]{1,0:T(8,128)(2,1)} %bitcast.75), channel_id=1, source_target_pairs={{0,2},{1,3},{2,0},{3,1},{4,6},{5,7},{6,4},{7,5},{8,10},{9,11},{10,... | collective-permute-start | bytes 196616 | tf_op jit(solution)/shard_map/ppermute | solution.py:24
  5.1 6.2 %collective-permute-start.2 = (bf16[16,2048]{1,0:T(8,128)(2,1)}, bf16[16,2048]{1,0:T(8,128)(2,1)S(1)}, u32[]{:S(2)}, u32[]{:S(2)}) collective-permute-start(bf16[16,2048]{1,0:T(8,128)(2,1)} %bitcast.76), channel_id=1, source_target_pairs={{0,1},{1,0},{2,3},{3,2},{4,5},{5,4},{6,7},{7,6},{8,9},{9,8},{10,11... | collective-permute-start | bytes 196616 | tf_op jit(solution)/shard_map/ppermute | solution.py:24
  5.7 5.6 %copy-start.1 = (bf16[1,16,2048]{2,1,0:T(8,128)(2,1)S(1)}, bf16[1,16,2048]{2,1,0:T(8,128)(2,1)}, u32[]{:S(2)}) copy-start(bf16[1,16,2048]{2,1,0:T(8,128)(2,1)} %param.12) | copy-start | bytes 196612
  11.3 5.8 %copy-start.3 = (s32[64,128]{1,0:T(8,128)S(1)}, s32[64,128]{1,0:T(8,128)}, u32[]{:S(2)}) copy-start(s32[64,128]{1,0:T(8,128)} %param.16) | copy-start | bytes 98308
  11.3 7.0 %copy-start.4 = (s32[1,16]{1,0:T(1,128)S(1)}, s32[1,16]{1,0:T(1,128)}, u32[]{:S(2)}) copy-start(s32[1,16]{1,0:T(1,128)} %param.15) | copy-start | bytes 196
  11.3 7.1 %copy-start.6 = (f32[64]{0:T(128)S(1)}, f32[64]{0:T(128)}, u32[]{:S(2)}) copy-start(f32[64]{0:T(128)} %constant.206.clone) | copy-start | bytes 772
  13.6 5.6 %collective-permute-start.3 = (bf16[16,2688]{1,0:T(8,128)(2,1)S(1)}, bf16[16,2688]{1,0:T(8,128)(2,1)S(1)}, u32[]{:S(2)}, u32[]{:S(2)}) collective-permute-start(bf16[16,2688]{1,0:T(8,128)(2,1)S(1)} %get-tuple-element.66), channel_id=1, source_target_pairs={{0,12},{4,8},{8,4},{12,0},{1,13},{5,9},{9,5},{13,1},{2,14},{6,10},... | collective-permute-start | bytes 258056 | tf_op jit(solution)/shard_map/ppermute | solution.py:24
  16.2 4.5 %collective-permute-start.4 = (bf16[16,2688]{1,0:T(8,128)(2,1)S(1)}, bf16[16,2688]{1,0:T(8,128)(2,1)S(1)}, u32[]{:S(2)}, u32[]{:S(2)}) collective-permute-start(bf16[16,2688]{1,0:T(8,128)(2,1)S(1)} %get-tuple-element.67), channel_id=1, source_target_pairs={{0,8},{4,12},{8,0},{12,4},{1,9},{5,13},{9,1},{13,5},{2,10},{6,14},... | collective-permute-start | bytes 258056 | tf_op jit(solution)/shard_map/ppermute | solution.py:24
  16.7 4.5 %collective-permute-start.5 = (bf16[16,2688]{1,0:T(8,128)(2,1)S(1)}, bf16[16,2688]{1,0:T(8,128)(2,1)S(1)}, u32[]{:S(2)}, u32[]{:S(2)}) collective-permute-start(bf16[16,2688]{1,0:T(8,128)(2,1)S(1)} %get-tuple-element.68), channel_id=1, source_target_pairs={{0,4},{4,0},{8,12},{12,8},{1,5},{5,1},{9,13},{13,9},{2,6},{6,2},{1... | collective-permute-start | bytes 258056 | tf_op jit(solution)/shard_map/ppermute | solution.py:24
  23.4 7.1 %collective-permute-start.6 = (bf16[16,2048]{1,0:T(8,128)(2,1)S(1)}, bf16[16,2048]{1,0:T(8,128)(2,1)S(1)}, u32[]{:S(2)}, u32[]{:S(2)}) collective-permute-start(bf16[16,2048]{1,0:T(8,128)(2,1)S(1)} %bitcast.70), channel_id=1, source_target_pairs={{0,12},{4,8},{8,4},{12,0},{1,13},{5,9},{9,5},{13,1},{2,14},{6,10},... | collective-permute-start | bytes 196616 | tf_op jit(solution)/shard_map/ppermute | solution.py:24
  25.0 5.6 %collective-permute-start.7 = (bf16[16,2048]{1,0:T(8,128)(2,1)S(1)}, bf16[16,2048]{1,0:T(8,128)(2,1)S(1)}, u32[]{:S(2)}, u32[]{:S(2)}) collective-permute-start(bf16[16,2048]{1,0:T(8,128)(2,1)S(1)} %bitcast.71), channel_id=1, source_target_pairs={{0,8},{4,12},{8,0},{12,4},{1,9},{5,13},{9,1},{13,5},{2,10},{6,14},... | collective-permute-start | bytes 196616 | tf_op jit(solution)/shard_map/ppermute | solution.py:24
  25.6 5.0 %collective-permute-start.8 = (bf16[16,2048]{1,0:T(8,128)(2,1)S(1)}, bf16[16,2048]{1,0:T(8,128)(2,1)S(1)}, u32[]{:S(2)}, u32[]{:S(2)}) collective-permute-start(bf16[16,2048]{1,0:T(8,128)(2,1)S(1)} %bitcast.72), channel_id=1, source_target_pairs={{0,4},{4,0},{8,12},{12,8},{1,5},{5,1},{9,13},{13,9},{2,6},{6,2},{1... | collective-permute-start | bytes 196616 | tf_op jit(solution)/shard_map/ppermute | solution.py:24
  32.3 6.7 %collective-permute-start.9 = (bf16[16,2048]{1,0:T(8,128)(2,1)S(1)}, bf16[16,2048]{1,0:T(8,128)(2,1)S(1)}, u32[]{:S(2)}, u32[]{:S(2)}) collective-permute-start(bf16[16,2048]{1,0:T(8,128)(2,1)S(1)} %pad_maximum_fusion.5), channel_id=1, source_target_pairs={{0,3},{1,2},{2,1},{3,0},{4,7},{5,6},{6,5},{7,4},{8,11},{9,10},{10,... | collective-permute-start | bytes 196616 | tf_op jit(solution)/shard_map/ppermute | solution.py:24
  36.0 5.2 %collective-permute-start.10 = (bf16[16,2048]{1,0:T(8,128)(2,1)S(1)}, bf16[16,2048]{1,0:T(8,128)(2,1)S(1)}, u32[]{:S(2)}, u32[]{:S(2)}) collective-permute-start(bf16[16,2048]{1,0:T(8,128)(2,1)S(1)} %pad_maximum_fusion.6), channel_id=1, source_target_pairs={{0,2},{1,3},{2,0},{3,1},{4,6},{5,7},{6,4},{7,5},{8,10},{9,11},{10,... | collective-permute-start | bytes 196616 | tf_op jit(solution)/shard_map/ppermute | solution.py:24
  36.0 5.1 %collective-permute-start.11 = (bf16[16,2048]{1,0:T(8,128)(2,1)S(1)}, bf16[16,2048]{1,0:T(8,128)(2,1)S(1)}, u32[]{:S(2)}, u32[]{:S(2)}) collective-permute-start(bf16[16,2048]{1,0:T(8,128)(2,1)S(1)} %pad_maximum_fusion.7), channel_id=1, source_target_pairs={{0,1},{1,0},{2,3},{3,2},{4,5},{5,4},{6,7},{7,6},{8,9},{9,8},{10,11... | collective-permute-start | bytes 196616 | tf_op jit(solution)/shard_map/ppermute | solution.py:24
  41.2 1.3 %collective-permute-start.12 = (bf16[8,2048]{1,0:T(8,128)(2,1)S(1)}, bf16[8,2048]{1,0:T(8,128)(2,1)S(1)}, u32[]{:S(2)}, u32[]{:S(2)}) collective-permute-start(bf16[8,2048]{1,0:T(8,128)(2,1)S(1)} %get-tuple-element.61), channel_id=1, source_target_pairs={{0,16},{16,0},{1,17},{17,1},{2,18},{18,2},{3,19},{19,3},{4,20},{20... | collective-permute-start | bytes 98312 | tf_op jit(solution)/shard_map/ppermute | solution.py:24
  42.5 5.2 %collective-permute-start.13 = (bf16[16,2048]{1,0:T(8,128)(2,1)S(1)}, bf16[16,2048]{1,0:T(8,128)(2,1)S(1)}, u32[]{:S(2)}, u32[]{:S(2)}) collective-permute-start(bf16[16,2048]{1,0:T(8,128)(2,1)S(1)} %pad_maximum_fusion.8), channel_id=1, source_target_pairs={{0,12},{4,8},{8,4},{12,0},{1,13},{5,9},{9,5},{13,1},{2,14},{6,10},... | collective-permute-start | bytes 196616 | tf_op jit(solution)/shard_map/ppermute | solution.py:24
  44.3 4.7 %collective-permute-start.14 = (bf16[16,2048]{1,0:T(8,128)(2,1)S(1)}, bf16[16,2048]{1,0:T(8,128)(2,1)S(1)}, u32[]{:S(2)}, u32[]{:S(2)}) collective-permute-start(bf16[16,2048]{1,0:T(8,128)(2,1)S(1)} %pad_maximum_fusion.8), channel_id=1, source_target_pairs={{0,8},{4,12},{8,0},{12,4},{1,9},{5,13},{9,1},{13,5},{2,10},{6,14},... | collective-permute-start | bytes 196616 | tf_op jit(solution)/shard_map/ppermute | solution.py:24
  44.8 4.3 %collective-permute-start.15 = (bf16[16,2048]{1,0:T(8,128)(2,1)S(1)}, bf16[16,2048]{1,0:T(8,128)(2,1)S(1)}, u32[]{:S(2)}, u32[]{:S(2)}) collective-permute-start(bf16[16,2048]{1,0:T(8,128)(2,1)S(1)} %pad_maximum_fusion.8), channel_id=1, source_target_pairs={{0,4},{4,0},{8,12},{12,8},{1,5},{5,1},{9,13},{13,9},{2,6},{6,2},{1... | collective-permute-start | bytes 196616 | tf_op jit(solution)/shard_map/ppermute | solution.py:24
  49.6 8.0 %collective-permute-start.16 = (bf16[8,8192]{1,0:T(8,128)(2,1)S(1)}, bf16[8,8192]{1,0:T(8,128)(2,1)S(1)}, u32[]{:S(2)}, u32[]{:S(2)}) collective-permute-start(bf16[8,8192]{1,0:T(8,128)(2,1)S(1)} %multiply_convert_fusion.refs_0_), channel_id=1, source_target_pairs={{0,1},{1,0},{2,3},{3,2},{4,5},{5,4},{6,7},{7,6},{8,9},{9,8},{10,11... | collective-permute-start | bytes 393224 | tf_op jit(solution)/shard_map/ppermute | solution.py:24
  50.2 12.7 %collective-permute-start.17 = (bf16[8,8192]{1,0:T(8,128)(2,1)S(1)}, bf16[8,8192]{1,0:T(8,128)(2,1)S(1)}, u32[]{:S(2)}, u32[]{:S(2)}) collective-permute-start(bf16[8,8192]{1,0:T(8,128)(2,1)S(1)} %multiply_convert_fusion.refs_0_), channel_id=1, source_target_pairs={{0,2},{1,3},{2,0},{3,1},{4,6},{5,7},{6,4},{7,5},{8,10},{9,11},{10,... | collective-permute-start | bytes 393224 | tf_op jit(solution)/shard_map/ppermute | solution.py:24
  51.9 11.0 %collective-permute-start.18 = (bf16[8,8192]{1,0:T(8,128)(2,1)S(1)}, bf16[8,8192]{1,0:T(8,128)(2,1)S(1)}, u32[]{:S(2)}, u32[]{:S(2)}) collective-permute-start(bf16[8,8192]{1,0:T(8,128)(2,1)S(1)} %multiply_convert_fusion.refs_0_), channel_id=1, source_target_pairs={{0,3},{1,2},{2,1},{3,0},{4,7},{5,6},{6,5},{7,4},{8,11},{9,10},{10,... | collective-permute-start | bytes 393224 | tf_op jit(solution)/shard_map/ppermute | solution.py:24
  (3 other events, 8.1 us)
where the time goes:
time: 78.9 us; the launch traced here: 78.8 us
  starting transfers between devices  25.3 us (32%)
  Pallas kernels  18.1 us (23%)
  waiting for transfers between devices  16 us (20%)
  blocking collectives  12.9 us (16%)
  other arithmetic  3.28 us (4%)
  matrix products  1.46 us (2%)
  between operations  0.91 us (1%)
  local copies, waits for them, and re-layouts  0.86 us (1%)
    ppermute x19, starting transfers between devices, swap(): return lax.ppermute(value, axis, pairs)  25.3 us
    ppermute x19, waiting for transfers between devices, swap(): return lax.ppermute(value, axis, pairs)  16 us
    all_to_all x1, blocking collectives, sum_totals(): return jnp.sum(lax.all_to_all(copies, axes, 0, 0, tiled=True), 0)  12.9 us
    pallas_call x2, Pallas kernels, load_to_vmem(): pl.pallas_call(load_kernel, out_shape=pltpu.VMEM(weight.shape, weight.dty...  7 us
    pallas_call x1, Pallas kernels, load_projections(): pl.pallas_call(load_projections_kernel, out_shape=(pltpu.VMEM(query.shape...  5.52 us
    pallas_call x2, Pallas kernels, matmul(): pl.pallas_call(lambda *refs: matmul_kernel(len(blocks), *refs), out_shape...  3.49 us
    pallas_call x1, Pallas kernels, head(): pl.pallas_call(head_kernel, out_shape=jax.ShapeDtypeStruct((rows, cols),...  2.06 us
  transfers between devices with their start and end apart: 19, of which 10 were waited for; matrix products, arithmetic and copies ran while one was open for 2% of the time, Pallas kernels for 16%

commit v1 on v0

--- a/solution.py
+++ b/solution.py
@@ -121,6 +121,33 @@
             flops=0, bytes_accessed=4 * weight.size, transcendentals=0
         ),
     )(pltpu.with_memory_space_constraint(weight, pltpu.HBM))
+
+
+def load_in_turn(weight, stream, turn, held=None):
+    def kernel(stream_ref, weight_ref, *refs):
+        out_ref, sems = refs[-2:]
+
+        @pl.when(stream_ref[0] == turn)
+        def _():
+            load_kernel(weight_ref, out_ref, sems)
+
+    operands = [stream.reshape(1), pltpu.with_memory_space_constraint(weight, pltpu.HBM)]
+    specs = [pl.BlockSpec(memory_space=pltpu.SMEM), pl.BlockSpec(memory_space=pltpu.HBM)]
+    if held is not None:
+        operands.append(pltpu.with_memory_space_constraint(held, pltpu.VMEM))
+        specs.append(pl.BlockSpec(memory_space=pltpu.VMEM))
+    return pl.pallas_call(
+        kernel,
+        out_shape=pltpu.VMEM(weight.shape, weight.dtype),
+        in_specs=specs,
+        out_specs=pl.BlockSpec(memory_space=pltpu.VMEM),
+        scratch_shapes=[pltpu.SemaphoreType.DMA((4,))],
+        input_output_aliases={} if held is None else {2: 0},
+        compiler_params=pltpu.CompilerParams(vmem_limit_bytes=8 * 1024 * 1024),
+        cost_estimate=pl.CostEstimate(
+            flops=0, bytes_accessed=4 * weight.size, transcendentals=0
+        ),
+    )(*operands)
 
 
 def load_projections_kernel(query_ref, pair_ref, query_out, pair_out, pair_raw, sems):
@@ -335,10 +362,13 @@
     mixed = jnp.sum(whole * factors[:, :, None], 0) * gain.astype(jnp.float32)
     mixed = mixed.astype(jnp.bfloat16)
 
+    places = jnp.stack([(tensor ^ distance) * share for distance in range(tensors)])
+    w_head, mixed, places = lax.optimization_barrier((w_head, mixed, places))
+    held = load_in_turn(w_head, stream, streams - 1)
+    held, mixed = lax.optimization_barrier((held, mixed))
     mixed_blocks = [swap(mixed, "tensor", distance) for distance in range(tensors)]
-    w_head, _ = lax.optimization_barrier((w_head, mixed))
-    places = jnp.stack([(tensor ^ distance) * share for distance in range(tensors)])
-    guided = head(places.astype(jnp.int32), mixed_blocks, load_to_vmem(w_head), penalty)
+    held = load_in_turn(w_head, stream, 0, held)
+    guided = head(places.astype(jnp.int32), mixed_blocks, held, penalty)
     totals = sum_totals(jnp.sum(jnp.exp(guided), 1), ("dp", "tensor"))
     return guided - jnp.log(totals)[:, None]
 

time: 78.9 us -> 81.4 us (1.032)
  waiting for transfers between devices: 16 us -> 19.3 us
    pallas_call x0 -> x2, Pallas kernels: none -> 3.55 us  [load_in_turn(): pl.pallas_call(kernel, out_shape=pltpu.VMEM(weight.shape, weight.dtype),...]
    pallas_call x2 -> x1, Pallas kernels: 7 us -> 3.5 us  [load_to_vmem(): pl.pallas_call(load_kernel, out_shape=pltpu.VMEM(weight.shape, weight.dty...]
    ppermute x19, waiting for transfers between devices: 16 us -> 19.3 us  [swap(): return lax.ppermute(value, axis, pairs)]
    all_to_all x1, blocking collectives: 12.9 us -> 12.1 us  [sum_totals(): return jnp.sum(lax.all_to_all(copies, axes, 0, 0, tiled=True), 0)]
  transfers between devices with their start and end apart: 19 -> 19, of which waited for: 10 -> 11; matrix products, arithmetic and copies ran while one was open for 2% -> 1% of each run, Pallas kernels for 16% -> 15%
where the time goes in v1:
time: 81.4 us; the launch traced here: 81.3 us
  starting transfers between devices  25.2 us (31%)
  waiting for transfers between devices  19.3 us (24%)
  Pallas kernels  18.1 us (22%)
  blocking collectives  12.1 us (15%)
  other arithmetic  3.28 us (4%)
  matrix products  1.46 us (2%)
  between operations  0.95 us (1%)
  local copies, waits for them, and re-layouts  0.87 us (1%)
    ppermute x19, starting transfers between devices, swap(): return lax.ppermute(value, axis, pairs)  25.2 us
    ppermute x19, waiting for transfers between devices, swap(): return lax.ppermute(value, axis, pairs)  19.3 us
    all_to_all x1, blocking collectives, sum_totals(): return jnp.sum(lax.all_to_all(copies, axes, 0, 0, tiled=True), 0)  12.1 us
    pallas_call x1, Pallas kernels, load_projections(): pl.pallas_call(load_projections_kernel, out_shape=(pltpu.VMEM(query.shape...  5.52 us
    pallas_call x2, Pallas kernels, load_in_turn(): pl.pallas_call(kernel, out_shape=pltpu.VMEM(weight.shape, weight.dtype),...  3.55 us
    pallas_call x1, Pallas kernels, load_to_vmem(): pl.pallas_call(load_kernel, out_shape=pltpu.VMEM(weight.shape, weight.dty...  3.5 us
    pallas_call x2, Pallas kernels, matmul(): pl.pallas_call(lambda *refs: matmul_kernel(len(blocks), *refs), out_shape...  3.49 us
    pallas_call x1, Pallas kernels, head(): pl.pallas_call(head_kernel, out_shape=jax.ShapeDtypeStruct((rows, cols),...  2.06 us
  transfers between devices with their start and end apart: 19, of which 11 were waited for; matrix products, arithmetic and copies ran while one was open for 1% of the time, Pallas kernels for 15%

profile of v1, /device:TPU:0, one launch (start us, length us, event | category | flops | bytes accessed | tf_op | source)
XLA Modules:
  0.0 81.3 jit_solution(12755583434729274680)
XLA Ops:
  0.0 3.0 %collective-permute-start.2 = (bf16[16,2048]{1,0:T(8,128)(2,1)}, bf16[16,2048]{1,0:T(8,128)(2,1)S(1)}, u32[]{:S(2)}, u32[]{:S(2)}) collective-permute-start(bf16[16,2048]{1,0:T(8,128)(2,1)} %bitcast.75), channel_id=1, source_target_pairs={{0,1},{1,0},{2,3},{3,2},{4,5},{5,4},{6,7},{7,6},{8,9},{9,8},{10,11... | collective-permute-start | bytes 196616 | tf_op jit(solution)/shard_map/ppermute | solution.py:24
  3.0 2.6 %collective-permute-start.1 = (bf16[16,2048]{1,0:T(8,128)(2,1)}, bf16[16,2048]{1,0:T(8,128)(2,1)S(1)}, u32[]{:S(2)}, u32[]{:S(2)}) collective-permute-start(bf16[16,2048]{1,0:T(8,128)(2,1)} %bitcast.76), channel_id=1, source_target_pairs={{0,2},{1,3},{2,0},{3,1},{4,6},{5,7},{6,4},{7,5},{8,10},{9,11},{10,... | collective-permute-start | bytes 196616 | tf_op jit(solution)/shard_map/ppermute | solution.py:24
  5.6 5.5 %shard_map.118 = (bf16[2048,2048]{1,0:T(8,128)(2,1)S(1)}, bf16[2048,512]{1,0:T(8,128)(2,1)S(1)}) custom-call(bf16[2048,2048]{1,0:T(8,128)(2,1)} %query_ref, bf16[2048,2,256]{2,1,0:T(2,128)(2,1)} %pair_ref), custom_call_target="tpu_custom_call" | custom-call | bytes 20971520 | tf_op jit(solution)/shard_map/pallas_call | solution.py:182
  11.9 1.9 %shard_map.119 = bf16[64,2560]{1,0:T(8,128)(2,1)S(1)} custom-call(bf16[16,2048]{1,0:T(8,128)(2,1)S(1)} %collective-permute-done.refs_0_, bf16[16,2048]{1,0:T(8,128)(2,1)S(1)} %collective-permute-done.1.refs_1_, bf16[16,2048]{1,0:T(8,128)(2,1)S(1)} %collective-permute-done.2.refs_2_, bf16[16,2048]{1,0:T(8,128)(2,1)S(1)} %bitcast.78, ...), custom_call_target="tpu_custom_call" | custom-call | flops 671088640 | bytes 11075584 | tf_op jit(solution)/shard_map/pallas_call | solution.py:57
  15.8 2.5 %collective-permute-start.3 = (bf16[16,2688]{1,0:T(8,128)(2,1)S(1)}, bf16[16,2688]{1,0:T(8,128)(2,1)S(1)}, u32[]{:S(2)}, u32[]{:S(2)}) collective-permute-start(bf16[16,2688]{1,0:T(8,128)(2,1)S(1)} %get-tuple-element.74), channel_id=1, source_target_pairs={{0,12},{4,8},{8,4},{12,0},{1,13},{5,9},{9,5},{13,1},{2,14},{6,10},... | collective-permute-start | bytes 258056 | tf_op jit(solution)/shard_map/ppermute | solution.py:24
  19.7 2.5 %collective-permute-done.3 = bf16[16,2688]{1,0:T(8,128)(2,1)S(1)} collective-permute-done((bf16[16,2688]{1,0:T(8,128)(2,1)S(1)}, bf16[16,2688]{1,0:T(8,128)(2,1)S(1)}, u32[]{:S(2)}, u32[]{:S(2)}) %collective-permute-start.3) | collective-permute-done | bytes 86048 | tf_op jit(solution)/shard_map/ppermute | solution.py:24
  26.1 1.5 %collective-permute-start.7 = (bf16[16,2048]{1,0:T(8,128)(2,1)S(1)}, bf16[16,2048]{1,0:T(8,128)(2,1)S(1)}, u32[]{:S(2)}, u32[]{:S(2)}) collective-permute-start(bf16[16,2048]{1,0:T(8,128)(2,1)S(1)} %bitcast.72), channel_id=1, source_target_pairs={{0,8},{4,12},{8,0},{12,4},{1,9},{5,13},{9,1},{13,5},{2,10},{6,14},... | collective-permute-start | bytes 196616 | tf_op jit(solution)/shard_map/ppermute | solution.py:24
  27.7 1.4 %collective-permute-start.6 = (bf16[16,2048]{1,0:T(8,128)(2,1)S(1)}, bf16[16,2048]{1,0:T(8,128)(2,1)S(1)}, u32[]{:S(2)}, u32[]{:S(2)}) collective-permute-start(bf16[16,2048]{1,0:T(8,128)(2,1)S(1)} %bitcast.73), channel_id=1, source_target_pairs={{0,12},{4,8},{8,4},{12,0},{1,13},{5,9},{9,5},{13,1},{2,14},{6,10},... | collective-permute-start | bytes 196616 | tf_op jit(solution)/shard_map/ppermute | solution.py:24
  29.2 3.5 %shard_map.120.refs_4_ = bf16[2048,2048]{1,0:T(8,128)(2,1)S(1)} custom-call(bf16[2048,2048]{1,0:T(8,128)(2,1)} %weight_ref), custom_call_target="tpu_custom_call" | custom-call | bytes 16777216 | tf_op jit(solution)/shard_map/pallas_call | solution.py:113
  32.8 1.6 %shard_map.121 = bf16[64,2048]{1,0:T(8,128)(2,1)S(1)} custom-call(bf16[16,2048]{1,0:T(8,128)(2,1)S(1)} %collective-permute-done.6.refs_0_, bf16[16,2048]{1,0:T(8,128)(2,1)S(1)} %collective-permute-done.7.refs_1_, bf16[16,2048]{1,0:T(8,128)(2,1)S(1)} %collective-permute-done.8.refs_2_, bf16[16,2048]{1,0:T(8,128)(2,1)S(1)} %bitcast.74, ...), custom_call_target="tpu_custom_call" | custom-call | flops 536870912 | bytes 8912896 | tf_op jit(solution)/shard_map/pallas_call | solution.py:57
  34.5 3.2 %collective-permute-start.9 = (bf16[16,2048]{1,0:T(8,128)(2,1)S(1)}, bf16[16,2048]{1,0:T(8,128)(2,1)S(1)}, u32[]{:S(2)}, u32[]{:S(2)}) collective-permute-start(bf16[16,2048]{1,0:T(8,128)(2,1)S(1)} %pad_maximum_fusion.5), channel_id=1, source_target_pairs={{0,3},{1,2},{2,1},{3,0},{4,7},{5,6},{6,5},{7,4},{8,11},{9,10},{10,... | collective-permute-start | bytes 196616 | tf_op jit(solution)/shard_map/ppermute | solution.py:24
  37.7 1.3 %collective-permute-start.11 = (bf16[16,2048]{1,0:T(8,128)(2,1)S(1)}, bf16[16,2048]{1,0:T(8,128)(2,1)S(1)}, u32[]{:S(2)}, u32[]{:S(2)}) collective-permute-start(bf16[16,2048]{1,0:T(8,128)(2,1)S(1)} %pad_maximum_fusion.7), channel_id=1, source_target_pairs={{0,1},{1,0},{2,3},{3,2},{4,5},{5,4},{6,7},{7,6},{8,9},{9,8},{10,11... | collective-permute-start | bytes 196616 | tf_op jit(solution)/shard_map/ppermute | solution.py:24
  39.0 1.7 %collective-permute-done.9 = bf16[16,2048]{1,0:T(8,128)(2,1)S(1)} collective-permute-done((bf16[16,2048]{1,0:T(8,128)(2,1)S(1)}, bf16[16,2048]{1,0:T(8,128)(2,1)S(1)}, u32[]{:S(2)}, u32[]{:S(2)}) %collective-permute-start.9) | collective-permute-done | bytes 65568 | tf_op jit(solution)/shard_map/ppermute | solution.py:24
  40.7 2.2 %collective-permute-done.10 = bf16[16,2048]{1,0:T(8,128)(2,1)S(1)} collective-permute-done((bf16[16,2048]{1,0:T(8,128)(2,1)S(1)}, bf16[16,2048]{1,0:T(8,128)(2,1)S(1)}, u32[]{:S(2)}, u32[]{:S(2)}) %collective-permute-start.10) | collective-permute-done | bytes 65568 | tf_op jit(solution)/shard_map/ppermute | solution.py:24
  44.2 1.4 %collective-permute-start.13 = (bf16[16,2048]{1,0:T(8,128)(2,1)S(1)}, bf16[16,2048]{1,0:T(8,128)(2,1)S(1)}, u32[]{:S(2)}, u32[]{:S(2)}) collective-permute-start(bf16[16,2048]{1,0:T(8,128)(2,1)S(1)} %pad_maximum_fusion.8), channel_id=1, source_target_pairs={{0,12},{4,8},{8,4},{12,0},{1,13},{5,9},{9,5},{13,1},{2,14},{6,10},... | collective-permute-start | bytes 196616 | tf_op jit(solution)/shard_map/ppermute | solution.py:24
  45.9 1.5 %collective-permute-start.15 = (bf16[16,2048]{1,0:T(8,128)(2,1)S(1)}, bf16[16,2048]{1,0:T(8,128)(2,1)S(1)}, u32[]{:S(2)}, u32[]{:S(2)}) collective-permute-start(bf16[16,2048]{1,0:T(8,128)(2,1)S(1)} %pad_maximum_fusion.8), channel_id=1, source_target_pairs={{0,4},{4,0},{8,12},{12,8},{1,5},{5,1},{9,13},{13,9},{2,6},{6,2},{1... | collective-permute-start | bytes 196616 | tf_op jit(solution)/shard_map/ppermute | solution.py:24
  48.0 1.5 %collective-permute-done.13 = bf16[16,2048]{1,0:T(8,128)(2,1)S(1)} collective-permute-done((bf16[16,2048]{1,0:T(8,128)(2,1)S(1)}, bf16[16,2048]{1,0:T(8,128)(2,1)S(1)}, u32[]{:S(2)}, u32[]{:S(2)}) %collective-permute-start.13) | collective-permute-done | bytes 65568 | tf_op jit(solution)/shard_map/ppermute | solution.py:24
  49.5 2.1 %collective-permute-done.14 = bf16[16,2048]{1,0:T(8,128)(2,1)S(1)} collective-permute-done((bf16[16,2048]{1,0:T(8,128)(2,1)S(1)}, bf16[16,2048]{1,0:T(8,128)(2,1)S(1)}, u32[]{:S(2)}, u32[]{:S(2)}) %collective-permute-start.14) | collective-permute-done | bytes 65568 | tf_op jit(solution)/shard_map/ppermute | solution.py:24
  52.2 2.2 %collective-permute-start.18 = (bf16[8,8192]{1,0:T(8,128)(2,1)S(1)}, bf16[8,8192]{1,0:T(8,128)(2,1)S(1)}, u32[]{:S(2)}, u32[]{:S(2)}) collective-permute-start(bf16[8,8192]{1,0:T(8,128)(2,1)S(1)} %multiply_convert_fusion.refs_0_), channel_id=1, source_target_pairs={{0,3},{1,2},{2,1},{3,0},{4,7},{5,6},{6,5},{7,4},{8,11},{9,10},{10,... | collective-permute-start | bytes 393224 | tf_op jit(solution)/shard_map/ppermute | solution.py:24
  54.4 2.3 %collective-permute-start.16 = (bf16[8,8192]{1,0:T(8,128)(2,1)S(1)}, bf16[8,8192]{1,0:T(8,128)(2,1)S(1)}, u32[]{:S(2)}, u32[]{:S(2)}) collective-permute-start(bf16[8,8192]{1,0:T(8,128)(2,1)S(1)} %multiply_convert_fusion.refs_0_), channel_id=1, source_target_pairs={{0,1},{1,0},{2,3},{3,2},{4,5},{5,4},{6,7},{7,6},{8,9},{9,8},{10,11... | collective-permute-start | bytes 393224 | tf_op jit(solution)/shard_map/ppermute | solution.py:24
  56.7 3.5 %shard_map.123.refs_4_ = bf16[8192,512]{1,0:T(8,128)(2,1)S(1)} custom-call(s32[1]{0:T(128)} %bitcast.22.stream_ref, bf16[8192,512]{1,0:T(8,128)(2,1)} %weight_ref.2, bf16[8192,512]{1,0:T(8,128)(2,1)S(1)} %shard_map.122.refs_0_), custom_call_target="tpu_custom_call", output_to_operand_aliasing={{}: (2, {})} | custom-call | bytes 16777216 | tf_op jit(solution)/shard_map/pallas_call | solution.py:139
  60.2 6.0 %collective-permute-done.17.refs_2_ = bf16[8,8192]{1,0:T(8,128)(2,1)S(1)} collective-permute-done((bf16[8,8192]{1,0:T(8,128)(2,1)S(1)}, bf16[8,8192]{1,0:T(8,128)(2,1)S(1)}, u32[]{:S(2)}, u32[]{:S(2)}) %collective-permute-start.17) | collective-permute-done | bytes 131104 | tf_op jit(solution)/shard_map/ppermute | solution.py:24
  66.2 2.1 %shard_map.124 = f32[32,512]{1,0:T(8,128)S(1)} custom-call(s32[4]{0:T(128)S(1)} %pad_add_fusion.places_ref, bf16[8,8192]{1,0:T(8,128)(2,1)S(1)} %multiply_convert_fusion.refs_0_, bf16[8,8192]{1,0:T(8,128)(2,1)S(1)} %collective-permute-done.16.refs_1_, bf16[8,8192]{1,0:T(8,128)(2,1)S(1)} %collective-permute-done.17.refs_2_, ...), custom_call_target="tpu_custom_call" | custom-call | flops 268435456 | bytes 9043968 | tf_op jit(solution)/shard_map/pallas_call | solution.py:85
  68.4 12.1 %all_to_all.6 = f32[16,1,32]{2,1,0:T(1,128)S(1)} all-to-all(f32[16,1,32]{2,1,0:T(1,128)S(1)} %broadcast_in_dim.22), channel_id=1, replica_groups=mesh['stream'=2,'dp'=4,'tensor'=4] {'dp','tensor'}, dimensions={0} | all-to-all | bytes 4096 | tf_op jit(solution)/shard_map/all_to_all | solution.py:38
  (95 shorter events, 11.2 us)
Async XLA Ops:
  0.0 24.1 %copy-start = (bf16[1,16,2,256,128]{4,3,2,1,0:T(8,128)(2,1)S(1)}, bf16[1,16,2,256,128]{4,3,2,1,0:T(8,128)(2,1)}, u32[]{:S(2)}) copy-start(bf16[1,16,2,256,128]{4,3,2,1,0:T(8,128)(2,1)} %param.13) | copy-start | bytes 6291460
  0.0 11.2 %collective-permute-start.2 = (bf16[16,2048]{1,0:T(8,128)(2,1)}, bf16[16,2048]{1,0:T(8,128)(2,1)S(1)}, u32[]{:S(2)}, u32[]{:S(2)}) collective-permute-start(bf16[16,2048]{1,0:T(8,128)(2,1)} %bitcast.75), channel_id=1, source_target_pairs={{0,1},{1,0},{2,3},{3,2},{4,5},{5,4},{6,7},{7,6},{8,9},{9,8},{10,11... | collective-permute-start | bytes 196616 | tf_op jit(solution)/shard_map/ppermute | solution.py:24
  3.0 8.1 %collective-permute-start.1 = (bf16[16,2048]{1,0:T(8,128)(2,1)}, bf16[16,2048]{1,0:T(8,128)(2,1)S(1)}, u32[]{:S(2)}, u32[]{:S(2)}) collective-permute-start(bf16[16,2048]{1,0:T(8,128)(2,1)} %bitcast.76), channel_id=1, source_target_pairs={{0,2},{1,3},{2,0},{3,1},{4,6},{5,7},{6,4},{7,5},{8,10},{9,11},{10,... | collective-permute-start | bytes 196616 | tf_op jit(solution)/shard_map/ppermute | solution.py:24
  5.6 6.3 %collective-permute-start = (bf16[16,2048]{1,0:T(8,128)(2,1)}, bf16[16,2048]{1,0:T(8,128)(2,1)S(1)}, u32[]{:S(2)}, u32[]{:S(2)}) collective-permute-start(bf16[16,2048]{1,0:T(8,128)(2,1)} %bitcast.77), channel_id=1, source_target_pairs={{0,3},{1,2},{2,1},{3,0},{4,7},{5,6},{6,5},{7,4},{8,11},{9,10},{10,... | collective-permute-start | bytes 196616 | tf_op jit(solution)/shard_map/ppermute | solution.py:24
  5.6 6.3 %copy-start.1 = (bf16[1,16,2048]{2,1,0:T(8,128)(2,1)S(1)}, bf16[1,16,2048]{2,1,0:T(8,128)(2,1)}, u32[]{:S(2)}) copy-start(bf16[1,16,2048]{2,1,0:T(8,128)(2,1)} %param.12) | copy-start | bytes 196612
  11.9 3.9 %copy-start.2 = (bf16[2048]{0:T(1024)(128)(2,1)S(1)}, bf16[2048]{0:T(1024)(128)(2,1)}, u32[]{:S(2)}) copy-start(bf16[2048]{0:T(1024)(128)(2,1)} %param.21) | copy-start | bytes 12292
  11.9 7.5 %copy-start.6 = (f32[64]{0:T(128)S(1)}, f32[64]{0:T(128)}, u32[]{:S(2)}) copy-start(f32[64]{0:T(128)} %constant.206.clone) | copy-start | bytes 772
  13.9 5.7 %copy-start.5 = (f32[64]{0:T(128)S(1)}, f32[64]{0:T(128)}, u32[]{:S(2)}) copy-start(f32[64]{0:T(128)} %param.17) | copy-start | bytes 772
  15.8 6.3 %collective-permute-start.3 = (bf16[16,2688]{1,0:T(8,128)(2,1)S(1)}, bf16[16,2688]{1,0:T(8,128)(2,1)S(1)}, u32[]{:S(2)}, u32[]{:S(2)}) collective-permute-start(bf16[16,2688]{1,0:T(8,128)(2,1)S(1)} %get-tuple-element.74), channel_id=1, source_target_pairs={{0,12},{4,8},{8,4},{12,0},{1,13},{5,9},{9,5},{13,1},{2,14},{6,10},... | collective-permute-start | bytes 258056 | tf_op jit(solution)/shard_map/ppermute | solution.py:24
  18.4 4.6 %collective-permute-start.4 = (bf16[16,2688]{1,0:T(8,128)(2,1)S(1)}, bf16[16,2688]{1,0:T(8,128)(2,1)S(1)}, u32[]{:S(2)}, u32[]{:S(2)}) collective-permute-start(bf16[16,2688]{1,0:T(8,128)(2,1)S(1)} %get-tuple-element.75), channel_id=1, source_target_pairs={{0,8},{4,12},{8,0},{12,4},{1,9},{5,13},{9,1},{13,5},{2,10},{6,14},... | collective-permute-start | bytes 258056 | tf_op jit(solution)/shard_map/ppermute | solution.py:24
  18.9 4.5 %collective-permute-start.5 = (bf16[16,2688]{1,0:T(8,128)(2,1)S(1)}, bf16[16,2688]{1,0:T(8,128)(2,1)S(1)}, u32[]{:S(2)}, u32[]{:S(2)}) collective-permute-start(bf16[16,2688]{1,0:T(8,128)(2,1)S(1)} %get-tuple-element.76), channel_id=1, source_target_pairs={{0,4},{4,0},{8,12},{12,8},{1,5},{5,1},{9,13},{13,9},{2,6},{6,2},{1... | collective-permute-start | bytes 258056 | tf_op jit(solution)/shard_map/ppermute | solution.py:24
  25.5 7.1 %collective-permute-start.8 = (bf16[16,2048]{1,0:T(8,128)(2,1)S(1)}, bf16[16,2048]{1,0:T(8,128)(2,1)S(1)}, u32[]{:S(2)}, u32[]{:S(2)}) collective-permute-start(bf16[16,2048]{1,0:T(8,128)(2,1)S(1)} %bitcast.71), channel_id=1, source_target_pairs={{0,4},{4,0},{8,12},{12,8},{1,5},{5,1},{9,13},{13,9},{2,6},{6,2},{1... | collective-permute-start | bytes 196616 | tf_op jit(solution)/shard_map/ppermute | solution.py:24
  26.1 6.6 %collective-permute-start.7 = (bf16[16,2048]{1,0:T(8,128)(2,1)S(1)}, bf16[16,2048]{1,0:T(8,128)(2,1)S(1)}, u32[]{:S(2)}, u32[]{:S(2)}) collective-permute-start(bf16[16,2048]{1,0:T(8,128)(2,1)S(1)} %bitcast.72), channel_id=1, source_target_pairs={{0,8},{4,12},{8,0},{12,4},{1,9},{5,13},{9,1},{13,5},{2,10},{6,14},... | collective-permute-start | bytes 196616 | tf_op jit(solution)/shard_map/ppermute | solution.py:24
  27.7 5.2 %collective-permute-start.6 = (bf16[16,2048]{1,0:T(8,128)(2,1)S(1)}, bf16[16,2048]{1,0:T(8,128)(2,1)S(1)}, u32[]{:S(2)}, u32[]{:S(2)}) collective-permute-start(bf16[16,2048]{1,0:T(8,128)(2,1)S(1)} %bitcast.73), channel_id=1, source_target_pairs={{0,12},{4,8},{8,4},{12,0},{1,13},{5,9},{9,5},{13,1},{2,14},{6,10},... | collective-permute-start | bytes 196616 | tf_op jit(solution)/shard_map/ppermute | solution.py:24
  34.5 6.1 %collective-permute-start.9 = (bf16[16,2048]{1,0:T(8,128)(2,1)S(1)}, bf16[16,2048]{1,0:T(8,128)(2,1)S(1)}, u32[]{:S(2)}, u32[]{:S(2)}) collective-permute-start(bf16[16,2048]{1,0:T(8,128)(2,1)S(1)} %pad_maximum_fusion.5), channel_id=1, source_target_pairs={{0,3},{1,2},{2,1},{3,0},{4,7},{5,6},{6,5},{7,4},{8,11},{9,10},{10,... | collective-permute-start | bytes 196616 | tf_op jit(solution)/shard_map/ppermute | solution.py:24
  37.7 5.2 %collective-permute-start.10 = (bf16[16,2048]{1,0:T(8,128)(2,1)S(1)}, bf16[16,2048]{1,0:T(8,128)(2,1)S(1)}, u32[]{:S(2)}, u32[]{:S(2)}) collective-permute-start(bf16[16,2048]{1,0:T(8,128)(2,1)S(1)} %pad_maximum_fusion.6), channel_id=1, source_target_pairs={{0,2},{1,3},{2,0},{3,1},{4,6},{5,7},{6,4},{7,5},{8,10},{9,11},{10,... | collective-permute-start | bytes 196616 | tf_op jit(solution)/shard_map/ppermute | solution.py:24
  37.7 5.1 %collective-permute-start.11 = (bf16[16,2048]{1,0:T(8,128)(2,1)S(1)}, bf16[16,2048]{1,0:T(8,128)(2,1)S(1)}, u32[]{:S(2)}, u32[]{:S(2)}) collective-permute-start(bf16[16,2048]{1,0:T(8,128)(2,1)S(1)} %pad_maximum_fusion.7), channel_id=1, source_target_pairs={{0,1},{1,0},{2,3},{3,2},{4,5},{5,4},{6,7},{7,6},{8,9},{9,8},{10,11... | collective-permute-start | bytes 196616 | tf_op jit(solution)/shard_map/ppermute | solution.py:24
  43.0 1.3 %collective-permute-start.12 = (bf16[8,2048]{1,0:T(8,128)(2,1)S(1)}, bf16[8,2048]{1,0:T(8,128)(2,1)S(1)}, u32[]{:S(2)}, u32[]{:S(2)}) collective-permute-start(bf16[8,2048]{1,0:T(8,128)(2,1)S(1)} %get-tuple-element.69), channel_id=1, source_target_pairs={{0,16},{16,0},{1,17},{17,1},{2,18},{18,2},{3,19},{19,3},{4,20},{20... | collective-permute-start | bytes 98312 | tf_op jit(solution)/shard_map/ppermute | solution.py:24
  44.2 5.3 %collective-permute-start.13 = (bf16[16,2048]{1,0:T(8,128)(2,1)S(1)}, bf16[16,2048]{1,0:T(8,128)(2,1)S(1)}, u32[]{:S(2)}, u32[]{:S(2)}) collective-permute-start(bf16[16,2048]{1,0:T(8,128)(2,1)S(1)} %pad_maximum_fusion.8), channel_id=1, source_target_pairs={{0,12},{4,8},{8,4},{12,0},{1,13},{5,9},{9,5},{13,1},{2,14},{6,10},... | collective-permute-start | bytes 196616 | tf_op jit(solution)/shard_map/ppermute | solution.py:24
  45.9 5.8 %collective-permute-start.15 = (bf16[16,2048]{1,0:T(8,128)(2,1)S(1)}, bf16[16,2048]{1,0:T(8,128)(2,1)S(1)}, u32[]{:S(2)}, u32[]{:S(2)}) collective-permute-start(bf16[16,2048]{1,0:T(8,128)(2,1)S(1)} %pad_maximum_fusion.8), channel_id=1, source_target_pairs={{0,4},{4,0},{8,12},{12,8},{1,5},{5,1},{9,13},{13,9},{2,6},{6,2},{1... | collective-permute-start | bytes 196616 | tf_op jit(solution)/shard_map/ppermute | solution.py:24
  47.4 4.3 %collective-permute-start.14 = (bf16[16,2048]{1,0:T(8,128)(2,1)S(1)}, bf16[16,2048]{1,0:T(8,128)(2,1)S(1)}, u32[]{:S(2)}, u32[]{:S(2)}) collective-permute-start(bf16[16,2048]{1,0:T(8,128)(2,1)S(1)} %pad_maximum_fusion.8), channel_id=1, source_target_pairs={{0,8},{4,12},{8,0},{12,4},{1,9},{5,13},{9,1},{13,5},{2,10},{6,14},... | collective-permute-start | bytes 196616 | tf_op jit(solution)/shard_map/ppermute | solution.py:24
  52.2 8.0 %collective-permute-start.18 = (bf16[8,8192]{1,0:T(8,128)(2,1)S(1)}, bf16[8,8192]{1,0:T(8,128)(2,1)S(1)}, u32[]{:S(2)}, u32[]{:S(2)}) collective-permute-start(bf16[8,8192]{1,0:T(8,128)(2,1)S(1)} %multiply_convert_fusion.refs_0_), channel_id=1, source_target_pairs={{0,3},{1,2},{2,1},{3,0},{4,7},{5,6},{6,5},{7,4},{8,11},{9,10},{10,... | collective-permute-start | bytes 393224 | tf_op jit(solution)/shard_map/ppermute | solution.py:24
  54.4 11.8 %collective-permute-start.17 = (bf16[8,8192]{1,0:T(8,128)(2,1)S(1)}, bf16[8,8192]{1,0:T(8,128)(2,1)S(1)}, u32[]{:S(2)}, u32[]{:S(2)}) collective-permute-start(bf16[8,8192]{1,0:T(8,128)(2,1)S(1)} %multiply_convert_fusion.refs_0_), channel_id=1, source_target_pairs={{0,2},{1,3},{2,0},{3,1},{4,6},{5,7},{6,4},{7,5},{8,10},{9,11},{10,... | collective-permute-start | bytes 393224 | tf_op jit(solution)/shard_map/ppermute | solution.py:24
  54.4 11.8 %collective-permute-start.16 = (bf16[8,8192]{1,0:T(8,128)(2,1)S(1)}, bf16[8,8192]{1,0:T(8,128)(2,1)S(1)}, u32[]{:S(2)}, u32[]{:S(2)}) collective-permute-start(bf16[8,8192]{1,0:T(8,128)(2,1)S(1)} %multiply_convert_fusion.refs_0_), channel_id=1, source_target_pairs={{0,1},{1,0},{2,3},{3,2},{4,5},{5,4},{6,7},{7,6},{8,9},{9,8},{10,11... | collective-permute-start | bytes 393224 | tf_op jit(solution)/shard_map/ppermute | solution.py:24
  (3 other events, 6.6 us)
